TPU v7x, 512 devices: a whole 4x8x8 slice. The times are simulated.
512 devices in a mesh: traj: 32 (over x, y), cand: 16 (over z, core).
Axes of the slice: x: 4, y: 8, z: 8, core: 2. Of those that a mesh axis runs over, the one named last changes fastest.
Arguments:
- state: float32 [4096, 256], P('traj'), may hold values from -6 to 6
- target: float32 [4096, 256], P('traj'), may hold values from -6 to 6
- coeffs: bfloat16 [33280, 256], P('cand'), may hold values from -6 to 6
- pairs: int32 [2, 33280], P(None, 'cand'), may hold values from 0 to 256, as said below
- mask: int32 [33280, 256], P('cand'), may hold values 0 or 1
Outputs:
- slope: float32 [4096, 256], P('traj')
- new_coeffs: bfloat16 [33280, 256], P('cand')
Inputs may be any that keep to these rules, and one draw needn't show every extreme that they name: Each column holds a pair pairs[0, c] <= pairs[1, c]; index 256 stands for the constant 1; no pair repeats before every pair has appeared.
All inputs are finite; a program needn't handle non-finite values. No bound on the sum of `mask` on one device may be relied on, other than what follows from the above.
Results may differ from a plain program's by a relative error of at most 0.014.
Values may be sent and summed in bfloat16 or wider, within the bound.
No kernel may reach another device: no remote copies, remote signals or barrier semaphores. Data moves between devices by JAX's collectives and lax.ppermute only.
A program may use at most 64 MiB of HBM per device.

v0:
```python
import math
import jax
import jax.numpy as jnp
from jax import lax
from jax.sharding import PartitionSpec as P

CANDS = 33280
step_dt = 0.25


def body(state, target, coeffs, pairs, mask):
    rows, modes_count = state.shape
    left = pairs[0]
    right = pairs[1]
    scale = 1.0 / math.sqrt(CANDS)
    segments = rows * lax.axis_size("traj")
    modes = jnp.arange(modes_count, dtype=jnp.int32)
    jac_left = (left[:, None] == modes[None, :]).astype(jnp.bfloat16)
    jac_right = (right[:, None] == modes[None, :]).astype(jnp.bfloat16)
    ones_col = jnp.ones((rows, 1), jnp.float32)

    def factors(y):
        z = jnp.concatenate([y, ones_col], 1)
        return (jnp.take(z, left, axis=1), jnp.take(z, right, axis=1))

    def library(y):
        left_vals, right_vals = factors(y)
        return (left_vals * right_vals).astype(jnp.bfloat16)

    def derive(theta):
        partial_rate = jnp.dot(theta, coeffs, preferred_element_type=jnp.float32) * scale
        return lax.psum(partial_rate, "cand")

    def pullback(cot, y):
        hidden = (
            lax.dot_general(
                cot.astype(jnp.bfloat16),
                coeffs,
                (((1,), (1,)), ((), ())),
                preferred_element_type=jnp.float32,
            )
            * scale
        )
        left_vals, right_vals = factors(y)
        upper = (hidden * right_vals).astype(jnp.bfloat16)
        lower = (hidden * left_vals).astype(jnp.bfloat16)
        partial_cot = jnp.dot(upper, jac_left, preferred_element_type=jnp.float32)
        partial_cot = partial_cot + jnp.dot(lower, jac_right, preferred_element_type=jnp.float32)
        return lax.psum(partial_cot, "cand")

    y_two = None
    th1 = library(state)
    k1 = derive(th1)
    y_two = state + 0.5 * step_dt * k1
    th2 = library(y_two)
    k2 = derive(th2)
    y_three = state + 0.5 * step_dt * k2
    th3 = library(y_three)
    k3 = derive(th3)
    y_four = state + step_dt * k3
    th4 = library(y_four)
    k4 = derive(th4)
    slope = (k1 + 2.0 * k2 + 2.0 * k3 + k4) / 6.0
    cot = (state + step_dt * slope - target) / segments
    g4 = step_dt / 6.0 * cot
    c4 = pullback(g4, y_four)
    g3 = step_dt / 3.0 * cot + step_dt * c4
    c3 = pullback(g3, y_three)
    g2 = step_dt / 3.0 * cot + 0.5 * step_dt * c3
    c2 = pullback(g2, y_two)
    g1 = step_dt / 6.0 * cot + 0.5 * step_dt * c2

    def outer(theta, grad_cot):
        return lax.dot_general(
            theta,
            grad_cot.astype(jnp.bfloat16),
            (((0,), (0,)), ((), ())),
            preferred_element_type=jnp.float32,
        )

    grad = (outer(th1, g1) + outer(th2, g2) + outer(th3, g3) + outer(th4, g4)) * scale
    rate = 0.5 * math.sqrt(segments * CANDS) / step_dt
    total = lax.psum(grad, "traj")
    fresh = (mask.astype(jnp.float32) * (coeffs.astype(jnp.float32) - rate * total)).astype(
        jnp.bfloat16
    )
    return (slope, fresh)


def solution(mesh):
    placed = (P("traj", None), P("traj", None), P("cand", None), P(None, "cand"), P("cand", None))
    return jax.shard_map(
        body,
        mesh=mesh,
        in_specs=placed,
        out_specs=(P("traj", None), P("cand", None)),
        check_vma=False,
    )
```

profile of v0, /device:TPU:16, one launch (start us, length us, event | category | flops | bytes accessed | tf_op | source)
XLA Modules:
  0.0 1064.3 jit_solution(13873290852304407379)
XLA Ops:
  7.2 0.8 slice_reduce_fusion.1
  8.1 1.0 copy.7
  9.1 3.9 gather_fusion.1
  13.1 5.1 gather_fusion
  18.2 3.0 fusion.19
  21.2 1.0 convolution_multiply_fusion.6
  22.2 118.2 %all-reduce.13.cloned.1.call-done = f32[128,256]{1,0:T(8,128)} async-done(((f32[128,256]{1,0:T(8,128)}), f32[128,256]{1,0:T(8,128)}) %all-reduce.13.cloned.1.call-update) | async-done | bytes 131088 | tf_op jit(solution)/shard_map/psum | solution.py:32
  140.4 0.9 multiply_add_fusion.2
  141.5 3.9 gather_fusion.3
  145.4 3.9 gather_fusion.2
  149.4 1.4 fusion.16
  150.8 0.8 copy-done.5
  151.6 1.0 convolution_multiply_fusion.5
  152.7 113.5 %all-reduce.15.cloned.1.call-done = f32[128,256]{1,0:T(8,128)} async-done(((f32[128,256]{1,0:T(8,128)}), f32[128,256]{1,0:T(8,128)}) %all-reduce.15.cloned.1.call-update) | async-done | bytes 131088 | tf_op jit(solution)/shard_map/psum | solution.py:32
  266.2 0.9 multiply_add_fusion.1
  267.9 0.9 concatenate.17.clone
  268.8 5.1 gather_fusion.5
  273.9 5.0 gather_fusion.4
  278.9 3.1 fusion.13
  282.0 0.8 copy-done.6
  282.8 1.0 convolution_multiply_fusion.4
  283.9 113.5 %all-reduce.17.cloned.1.call-done = f32[128,256]{1,0:T(8,128)} async-done(((f32[128,256]{1,0:T(8,128)}), f32[128,256]{1,0:T(8,128)}) %all-reduce.17.cloned.1.call-update) | async-done | bytes 131088 | tf_op jit(solution)/shard_map/psum | solution.py:32
  397.4 0.9 multiply_add_fusion
  399.1 0.9 concatenate.18.clone
  400.0 5.1 gather_fusion.7
  405.1 5.0 gather_fusion.6
  410.1 3.1 fusion.10
  413.2 0.8 copy-done.8
  414.0 1.0 convolution_multiply_fusion.3
  415.1 113.5 %all-reduce.19.cloned.1.call-done = f32[128,256]{1,0:T(8,128)} async-done(((f32[128,256]{1,0:T(8,128)}), f32[128,256]{1,0:T(8,128)}) %all-reduce.19.cloned.1.call-update) | async-done | bytes 131088 | tf_op jit(solution)/shard_map/psum | solution.py:32
  528.6 1.9 add_subtract_fusion
  530.9 0.8 copy-done.4
  531.7 1.0 fusion.3
  532.9 1.7 fusion.7
  534.7 113.5 %all-reduce.21.cloned.1.call-done = f32[128,256]{1,0:T(8,128)} async-done(((f32[128,256]{1,0:T(8,128)}), f32[128,256]{1,0:T(8,128)}) %all-reduce.21.cloned.1.call-update) | async-done | bytes 131088 | tf_op jit(solution)/shard_map/psum | solution.py:49
  648.2 0.9 add_convert_fusion.2
  650.4 1.0 fusion.2
  651.6 1.7 fusion.8
  653.5 113.3 %all-reduce.23.cloned.1.call-done = f32[128,256]{1,0:T(8,128)} async-done(((f32[128,256]{1,0:T(8,128)}), f32[128,256]{1,0:T(8,128)}) %all-reduce.23.cloned.1.call-update) | async-done | bytes 131088 | tf_op jit(solution)/shard_map/psum | solution.py:49
  766.9 0.9 add_convert_fusion.1
  768.2 1.0 fusion.1
  769.2 1.7 fusion.9
  771.0 113.5 %all-reduce.25.cloned.1.call-done = f32[128,256]{1,0:T(8,128)} async-done(((f32[128,256]{1,0:T(8,128)}), f32[128,256]{1,0:T(8,128)}) %all-reduce.25.cloned.1.call-update) | async-done | bytes 131088 | tf_op jit(solution)/shard_map/psum | solution.py:49
  884.5 1.3 fusion.44
  885.8 1.5 convolution_add_fusion.2
  888.4 1.8 fusion
  890.9 163.6 %all-reduce.27.cloned.1.call-done = f32[2080,256]{1,0:T(8,128)} async-done(((f32[2080,256]{1,0:T(8,128)}), f32[2080,256]{1,0:T(8,128)}) %all-reduce.27.cloned.1.call-update) | async-done | bytes 2129936 | tf_op jit(solution)/shard_map/psum | solution.py:83
  1054.5 3.0 multiply_convert_fusion
  (56 shorter events, 6.6 us)
Async XLA Ops:
  7.2 133.3 %all-reduce.13.cloned.1.call-start = ((), (), s32[]{:S(2)}) async-start(), calls=%async_computation | async-start | bytes 262144 | tf_op jit(solution)/shard_map/psum | solution.py:32
  18.1 3.0 copy-start
  21.1 120.2 %copy-start.10 = (bf16[128,2080]{0,1:T(8,128)(2,1)}, bf16[128,2080]{0,1:T(8,128)(2,1)S(1)}, u32[]{:S(2)}) copy-start(bf16[128,2080]{0,1:T(8,128)(2,1)S(1)} %fusion.19) | copy-start | bytes 1597444
  21.1 119.3 %copy-start.12 = (f32[128,256]{1,0:T(8,128)S(1)}, f32[128,256]{1,0:T(8,128)}, u32[]{:S(2)}) copy-start(f32[128,256]{1,0:T(8,128)} %param.7) | copy-start | bytes 393220
  22.2 244.0 %all-reduce.15.cloned.1.call-start = ((), (), s32[]{:S(2)}) async-start(), calls=%async_computation.1 | async-start | bytes 262144 | tf_op jit(solution)/shard_map/psum | solution.py:32
  150.8 0.8 copy-start.5
  152.6 244.8 %all-reduce.17.cloned.1.call-start = ((), (), s32[]{:S(2)}) async-start(), calls=%async_computation.2 | async-start | bytes 262144 | tf_op jit(solution)/shard_map/psum | solution.py:32
  282.0 0.8 copy-start.6
  283.8 244.8 %all-reduce.19.cloned.1.call-start = ((), (), s32[]{:S(2)}) async-start(), calls=%async_computation.3 | async-start | bytes 262144 | tf_op jit(solution)/shard_map/psum | solution.py:32
  413.2 0.8 copy-start.8
  415.0 233.2 %all-reduce.21.cloned.1.call-start = ((), (), s32[]{:S(2)}) async-start(), calls=%async_computation.4 | async-start | bytes 262144 | tf_op jit(solution)/shard_map/psum | solution.py:49
  530.5 1.2 copy-start.4
  531.7 1.2 copy-start.3
  534.6 232.2 %all-reduce.23.cloned.1.call-start = ((), (), s32[]{:S(2)}) async-start(), calls=%async_computation.5 | async-start | bytes 262144 | tf_op jit(solution)/shard_map/psum | solution.py:49
  649.1 1.2 copy-start.2
  650.4 1.2 copy-start.1
  653.3 231.2 %all-reduce.25.cloned.1.call-start = ((), (), s32[]{:S(2)}) async-start(), calls=%async_computation.6 | async-start | bytes 262144 | tf_op jit(solution)/shard_map/psum | solution.py:49
  769.2 115.3 %copy-start.11 = (bf16[128,2080]{0,1:T(8,128)(2,1)S(1)}, bf16[128,2080]{0,1:T(8,128)(2,1)}, u32[]{:S(2)}) copy-start(bf16[128,2080]{0,1:T(8,128)(2,1)} %copy-done.10) | copy-start | bytes 1597444
  770.9 283.5 %all-reduce.27.cloned.1.call-start = ((), (), s32[]{:S(2)}) async-start(), calls=%async_computation.7 | async-start | bytes 4259840 | tf_op jit(solution)/shard_map/psum | solution.py:83
  885.8 1.5 copy-start.7
  887.4 1.0 copy-start.9
  888.4 1.8 copy-start.14
  890.2 164.3 %copy-start.13 = (s32[2080,256]{1,0:T(8,128)S(1)}, s32[2080,256]{1,0:T(8,128)}, u32[]{:S(2)}) copy-start(s32[2080,256]{1,0:T(8,128)} %param.11) | copy-start | bytes 6389764
Sparse Core Ops, SparseCore 0:
  22.3 118.0 all-reduce.12
  152.7 113.4 all-reduce.14
  284.0 113.4 all-reduce.16
  415.2 113.4 all-reduce.18
  534.8 113.4 all-reduce.20
  653.4 113.4 all-reduce.22
  771.0 113.3 all-reduce.24
  890.3 164.0 all-reduce.26
where the time goes:
time: 1060 us
  waiting for transfers between devices  963 us (91%)
  local copies, waits for them, and re-layouts  47.4 us (4%)
  other arithmetic  20.6 us (2%)
  matrix products  18.4 us (2%)
  between operations  14.5 us (1%)
    psum x4, waiting for transfers between devices, derive(): return lax.psum(partial_rate, 'cand')  459 us
    psum x3, waiting for transfers between devices, pullback(): return lax.psum(partial_cot, 'cand')  340 us
    psum x1, waiting for transfers between devices, body(): total = lax.psum(grad, 'traj')  164 us
    gather x8, local copies, waits for them, and re-layouts, factors(): return (jnp.take(z, left, axis=1), jnp.take(z, right, axis=1))  37.1 us
  transfers between devices with their start and end apart: 8, of which 8 were waited for; matrix products, arithmetic and copies ran while one was open for 0% of the time, Pallas kernels for 0%

commit v1 on v0

--- a/solution.py
+++ b/solution.py
@@ -29,7 +29,7 @@
 
     def derive(theta):
         partial_rate = jnp.dot(theta, coeffs, preferred_element_type=jnp.float32) * scale
-        return lax.psum(partial_rate, "cand")
+        return jnp.sum(lax.all_gather(partial_rate, "cand"), axis=0)
 
     def pullback(cot, y):
         hidden = (

time: 1060 us -> 785 us (0.74)
  waiting for transfers between devices: 963 us -> 674 us
    psum x4 -> x0, waiting for transfers between devices: 459 us -> none  [derive(): return lax.psum(partial_rate, 'cand')]
    all_gather x0 -> x4, waiting for transfers between devices: none -> 172 us  [derive(): return jnp.sum(lax.all_gather(partial_rate, 'cand'), axis=0)]
where the time goes in v1:
time: 785 us; the launch traced here: 784 us
  waiting for transfers between devices  674 us (86%)
  local copies, waits for them, and re-layouts  49.9 us (6%)
  other arithmetic  26.9 us (3%)
  matrix products  18.3 us (2%)
  between operations  14.5 us (2%)
    psum x3, waiting for transfers between devices, pullback(): return lax.psum(partial_cot, 'cand')  339 us
    all_gather x4, waiting for transfers between devices, derive(): return jnp.sum(lax.all_gather(partial_rate, 'cand'), axis=0)  172 us
    psum x1, waiting for transfers between devices, body(): total = lax.psum(grad, 'traj')  164 us
    gather x8, local copies, waits for them, and re-layouts, factors(): return (jnp.take(z, left, axis=1), jnp.take(z, right, axis=1))  37.1 us
  transfers between devices with their start and end apart: 8, of which 8 were waited for; matrix products, arithmetic and copies ran while one was open for 0% of the time, Pallas kernels for 0%

profile of v1, /device:TPU:16, one launch (start us, length us, event | category | flops | bytes accessed | tf_op | source)
XLA Modules:
  0.0 784.3 jit_solution(2606318454699575099)
XLA Ops:
  7.2 0.8 slice_reduce_fusion.1
  8.1 1.0 copy.7
  9.1 3.9 gather_fusion.1
  13.1 5.1 gather_fusion
  18.2 3.0 fusion.19
  21.1 1.0 convolution_multiply_fusion.6
  22.2 47.8 %all-gather.9.cloned.1.call-done = f32[2048,256]{1,0:T(8,128)} async-done(((f32[128,256]{1,0:T(8,128)}), f32[2048,256]{1,0:T(8,128)}) %all-gather.9.cloned.1.call-update) | async-done | bytes 2097168 | tf_op jit(solution)/shard_map/all_gather | solution.py:32
  70.0 1.8 reduce_sum.36
  72.5 3.9 gather_fusion.3
  76.5 3.9 gather_fusion.2
  80.5 1.4 fusion.16
  81.8 0.8 copy-done.5
  82.7 1.0 convolution_multiply_fusion.5
  83.8 41.4 %all-gather.11.cloned.1.call-done = f32[2048,256]{1,0:T(8,128)} async-done(((f32[128,256]{1,0:T(8,128)}), f32[2048,256]{1,0:T(8,128)}) %all-gather.11.cloned.1.call-update) | async-done | bytes 2097168 | tf_op jit(solution)/shard_map/all_gather | solution.py:32
  125.1 1.7 reduce_sum.37
  127.6 1.7 copy.15
  129.2 0.9 concatenate.17.clone
  130.1 5.1 gather_fusion.5
  135.2 5.0 gather_fusion.4
  140.2 3.1 fusion.13
  144.1 1.0 convolution_multiply_fusion.4
  145.2 41.4 %all-gather.13.cloned.1.call-done = f32[2048,256]{1,0:T(8,128)} async-done(((f32[128,256]{1,0:T(8,128)}), f32[2048,256]{1,0:T(8,128)}) %all-gather.13.cloned.1.call-update) | async-done | bytes 2097168 | tf_op jit(solution)/shard_map/all_gather | solution.py:32
  186.6 1.7 reduce_sum.38
  189.0 1.7 copy.16
  190.7 0.9 concatenate.18.clone
  191.6 5.0 gather_fusion.7
  196.7 5.1 gather_fusion.6
  201.7 3.1 fusion.10
  205.6 1.0 convolution_multiply_fusion.3
  206.7 41.4 %all-gather.15.cloned.1.call-done = f32[2048,256]{1,0:T(8,128)} async-done(((f32[128,256]{1,0:T(8,128)}), f32[2048,256]{1,0:T(8,128)}) %all-gather.15.cloned.1.call-update) | async-done | bytes 2097168 | tf_op jit(solution)/shard_map/all_gather | solution.py:32
  248.1 2.4 reduce_sum.39
  250.5 1.9 add_subtract_fusion
  253.6 1.0 fusion.3
  254.8 1.6 fusion.7
  256.5 111.8 %all-reduce.9.cloned.1.call-done = f32[128,256]{1,0:T(8,128)} async-done(((f32[128,256]{1,0:T(8,128)}), f32[128,256]{1,0:T(8,128)}) %all-reduce.9.cloned.1.call-update) | async-done | bytes 131088 | tf_op jit(solution)/shard_map/psum | solution.py:49
  368.3 0.9 add_convert_fusion.2
  370.4 1.0 fusion.2
  371.7 1.7 fusion.8
  373.6 113.3 %all-reduce.11.cloned.1.call-done = f32[128,256]{1,0:T(8,128)} async-done(((f32[128,256]{1,0:T(8,128)}), f32[128,256]{1,0:T(8,128)}) %all-reduce.11.cloned.1.call-update) | async-done | bytes 131088 | tf_op jit(solution)/shard_map/psum | solution.py:49
  486.9 0.9 add_convert_fusion.1
  488.3 1.0 fusion.1
  489.3 1.7 fusion.9
  491.0 113.5 %all-reduce.13.cloned.1.call-done = f32[128,256]{1,0:T(8,128)} async-done(((f32[128,256]{1,0:T(8,128)}), f32[128,256]{1,0:T(8,128)}) %all-reduce.13.cloned.1.call-update) | async-done | bytes 131088 | tf_op jit(solution)/shard_map/psum | solution.py:49
  604.6 1.3 fusion.44
  605.9 1.5 convolution_add_fusion.2
  608.5 1.8 fusion
  610.9 163.6 %all-reduce.15.cloned.1.call-done = f32[2080,256]{1,0:T(8,128)} async-done(((f32[2080,256]{1,0:T(8,128)}), f32[2080,256]{1,0:T(8,128)}) %all-reduce.15.cloned.1.call-update) | async-done | bytes 2129936 | tf_op jit(solution)/shard_map/psum | solution.py:83
  774.5 3.0 multiply_convert_fusion
  (66 shorter events, 9.4 us)
Async XLA Ops:
  7.2 62.8 %all-gather.9.cloned.1.call-start = ((), (), s32[]{:S(2)}) async-start(), calls=%async_computation.4 | async-start | bytes 2228224 | tf_op jit(solution)/shard_map/all_gather | solution.py:32
  18.1 3.0 copy-start
  21.1 50.6 %copy-start.10 = (bf16[128,2080]{0,1:T(8,128)(2,1)}, bf16[128,2080]{0,1:T(8,128)(2,1)S(1)}, u32[]{:S(2)}) copy-start(bf16[128,2080]{0,1:T(8,128)(2,1)S(1)} %fusion.19) | copy-start | bytes 1597444
  22.2 102.9 %all-gather.11.cloned.1.call-start = ((), (), s32[]{:S(2)}) async-start(), calls=%async_computation.5 | async-start | bytes 2228224 | tf_op jit(solution)/shard_map/all_gather | solution.py:32
  70.0 1.8 copy-start.12
  71.8 0.6 copy-start.14
  81.8 0.8 copy-start.5
  83.7 102.9 %all-gather.13.cloned.1.call-start = ((), (), s32[]{:S(2)}) async-start(), calls=%async_computation.6 | async-start | bytes 2228224 | tf_op jit(solution)/shard_map/all_gather | solution.py:32
  126.9 0.7 copy-start.15
  143.3 0.8 copy-start.6
  145.2 102.9 %all-gather.15.cloned.1.call-start = ((), (), s32[]{:S(2)}) async-start(), calls=%async_computation.7 | async-start | bytes 2228224 | tf_op jit(solution)/shard_map/all_gather | solution.py:32
  188.3 0.7 copy-start.16
  204.8 0.8 copy-start.8
  206.7 161.6 %all-reduce.9.cloned.1.call-start = ((), (), s32[]{:S(2)}) async-start(), calls=%async_computation | async-start | bytes 262144 | tf_op jit(solution)/shard_map/psum | solution.py:49
  252.3 1.2 copy-start.4
  253.6 1.2 copy-start.3
  256.5 230.5 %all-reduce.11.cloned.1.call-start = ((), (), s32[]{:S(2)}) async-start(), calls=%async_computation.1 | async-start | bytes 262144 | tf_op jit(solution)/shard_map/psum | solution.py:49
  369.2 1.2 copy-start.2
  370.4 1.2 copy-start.1
  373.3 231.2 %all-reduce.13.cloned.1.call-start = ((), (), s32[]{:S(2)}) async-start(), calls=%async_computation.2 | async-start | bytes 262144 | tf_op jit(solution)/shard_map/psum | solution.py:49
  489.3 115.3 %copy-start.11 = (bf16[128,2080]{0,1:T(8,128)(2,1)S(1)}, bf16[128,2080]{0,1:T(8,128)(2,1)}, u32[]{:S(2)}) copy-start(bf16[128,2080]{0,1:T(8,128)(2,1)} %copy-done.10) | copy-start | bytes 1597444
  491.0 283.5 %all-reduce.15.cloned.1.call-start = ((), (), s32[]{:S(2)}) async-start(), calls=%async_computation.3 | async-start | bytes 4259840 | tf_op jit(solution)/shard_map/psum | solution.py:83
  605.9 1.5 copy-start.7
  607.4 1.0 copy-start.9
  608.5 1.8 copy-start.17
  610.2 164.3 %copy-start.13 = (s32[2080,256]{1,0:T(8,128)S(1)}, s32[2080,256]{1,0:T(8,128)}, u32[]{:S(2)}) copy-start(s32[2080,256]{1,0:T(8,128)} %param.11) | copy-start | bytes 6389764
Sparse Core Ops, SparseCore 0:
  22.3 47.6 all-gather.8
  83.8 41.2 all-gather.10
  145.3 41.2 all-gather.12
  206.8 41.2 all-gather.14
  256.6 111.6 all-reduce.8
  373.5 113.4 all-reduce.10
  491.1 113.4 all-reduce.12
  610.4 164.1 all-reduce.14
